TPU v7x, 512 devices: a whole 4x4x16 slice. The times are simulated.
512 devices in a mesh: tile: 32 (over z, core), band: 4 (over x), pos: 4 (over y).
Axes of the slice: x: 4, y: 4, z: 16, core: 2. Of those that a mesh axis runs over, the one named last changes fastest.
Arguments:
- object_planes: float32 [2, 8192, 1024], P(None, 'tile', 'band'), may hold values from -6 to 6
- probe_planes: float32 [2, 2, 256, 256], replicated, may hold values from -6 to 6
- patterns: float32 [32, 4, 4, 3, 256, 256], P('tile', 'band', 'pos'), may hold values from 0.5 to 8
- offsets: int32 [32, 4, 4, 3, 2], P('tile', 'band', 'pos'), may hold values from 0 to 255, as said below
- counts: int32 [32, 4, 4], P('tile', 'band', 'pos'), may hold values from 0 to 3, as said below
Outputs:
- object_new: float32 [2, 8192, 1024], P(None, 'tile', 'band')
- probe_new: float32 [2, 2, 256, 256], replicated
Inputs may be any that keep to these rules, and one draw needn't show every extreme that they name: `offsets`: corners lie inside their tile: rows below 256, columns below 256. Only the first counts[t, b, p] slots of a device hold positions; later slots are to be ignored. `counts`: each device holds at most 3 positions; in every tile one device along pos holds exactly 3, and the 4 devices of a tile hold exactly 8 positions together.
All inputs are finite; a program needn't handle non-finite values.
Results may differ from a plain program's by a relative error of at most 0.0003.
Values sent between devices are 32-bit elements; how exact they have to be, the bound alone decides.
No kernel may reach another device: no remote copies, remote signals or barrier semaphores. Data moves between devices by JAX's collectives and lax.ppermute only.
A program may use at most 192 MiB of HBM per device.

v0:
```python
import math
import jax
import jax.numpy as jnp
from jax import lax
from jax.sharding import PartitionSpec as P

precise = lax.Precision.HIGHEST


def shifted(block, axis, distance):
    devices = range(lax.axis_size(axis))
    route = [(i - distance, i) for i in devices if i - distance in devices]
    return lax.ppermute(block, axis, route)


def dft_tables(pixels):
    indices = jnp.arange(pixels, dtype=jnp.int32)
    phase = indices[:, None] * indices[None, :] % pixels
    angle = phase.astype(jnp.float32) * (2.0 * math.pi / pixels)
    factor = 1.0 / math.sqrt(pixels)
    return (jnp.cos(angle) * factor, jnp.sin(angle) * factor)


def transform(real_part, imag_part, cosine, sine_table, direction):
    left_real = jnp.einsum(
        "ij,nmjk->nmik", cosine, real_part, precision=precise
    ) + direction * jnp.einsum("ij,nmjk->nmik", sine_table, imag_part, precision=precise)
    left_imag = jnp.einsum(
        "ij,nmjk->nmik", cosine, imag_part, precision=precise
    ) - direction * jnp.einsum("ij,nmjk->nmik", sine_table, real_part, precision=precise)
    out_real = jnp.einsum(
        "nmij,jk->nmik", left_real, cosine, precision=precise
    ) + direction * jnp.einsum("nmij,jk->nmik", left_imag, sine_table, precision=precise)
    out_imag = jnp.einsum(
        "nmij,jk->nmik", left_imag, cosine, precision=precise
    ) - direction * jnp.einsum("nmij,jk->nmik", left_real, sine_table, precision=precise)
    return (out_real, out_imag)


def on_device(object_planes, probe_planes, patterns, offsets, counts):
    pixels = probe_planes.shape[-1]
    capacity = patterns.shape[3]
    tile_rows = object_planes.shape[1]
    tile_cols = object_planes.shape[2]
    beside_cols = shifted(object_planes, "band", -1)
    widened = jnp.concatenate([object_planes, beside_cols], axis=2)
    below_rows = shifted(widened, "tile", -1)
    extended = jnp.concatenate([widened, below_rows], axis=1)
    local_count = counts.reshape(())
    frames = patterns[0, 0, 0]
    places = offsets[0, 0, 0]
    weights = (jnp.arange(capacity, dtype=jnp.int32) < local_count).astype(jnp.float32)
    slot_total = frames.shape[0]
    zero_index = jnp.int32(0)
    patches = jnp.stack(
        [
            lax.dynamic_slice(
                extended, (zero_index, places[number, 0], places[number, 1]), (2, pixels, pixels)
            )
            for number in range(slot_total)
        ]
    )
    patch_real = patches[:, 0][:, None]
    patch_imag = patches[:, 1][:, None]
    probe_real = probe_planes[0][None]
    probe_imag = probe_planes[1][None]
    wave_real = probe_real * patch_real - probe_imag * patch_imag
    wave_imag = probe_real * patch_imag + probe_imag * patch_real
    cosine, sine_table = dft_tables(pixels)
    far_real, far_imag = transform(wave_real, wave_imag, cosine, sine_table, 1.0)
    intensity = jnp.sum(far_real * far_real + far_imag * far_imag, axis=1)
    scaling = (jnp.sqrt(frames) / jnp.sqrt(intensity + 1.0))[:, None]
    back_real, back_imag = transform(
        far_real * scaling, far_imag * scaling, cosine, sine_table, -1.0
    )
    corr_real = back_real - wave_real
    corr_imag = back_imag - wave_imag
    slot_weight = weights[:, None, None]
    object_real = slot_weight * jnp.sum(probe_real * corr_real + probe_imag * corr_imag, axis=1)
    object_imag = slot_weight * jnp.sum(probe_real * corr_imag - probe_imag * corr_real, axis=1)
    probe_power = jnp.sum(probe_planes[0] ** 2 + probe_planes[1] ** 2, axis=0)
    lighting = slot_weight * probe_power[None]
    contributions = jnp.stack([object_real, object_imag, lighting], axis=1)
    plane_count = contributions.shape[1]
    running = jnp.zeros((plane_count, tile_rows + pixels, tile_cols + pixels), jnp.float32)
    for number in range(slot_total):
        corner_at = (zero_index, places[number, 0], places[number, 1])
        previous = lax.dynamic_slice(running, corner_at, (plane_count, pixels, pixels))
        running = lax.dynamic_update_slice(running, previous + contributions[number], corner_at)
    mode_weight = weights[:, None, None, None]
    numer_real = jnp.sum(mode_weight * (patch_real * corr_real + patch_imag * corr_imag), axis=0)
    numer_imag = jnp.sum(mode_weight * (patch_real * corr_imag - patch_imag * corr_real), axis=0)
    density = jnp.sum(slot_weight * (patches[:, 0] ** 2 + patches[:, 1] ** 2), axis=0)
    from_left = shifted(running[:, :, tile_cols:], "band", 1)
    column_core = running[:, :, :tile_cols].at[:, :, :pixels].add(from_left)
    from_above = shifted(column_core[:, tile_rows:, :], "tile", 1)
    tile_core = column_core[:, :tile_rows, :].at[:, :pixels, :].add(from_above)
    tile_total = lax.psum(tile_core, "pos")
    tile_light = tile_total[2]
    object_new = object_planes + tile_total[:2] / (tile_light + 1.0)
    sum_numer, sum_density = lax.psum(
        (jnp.stack([numer_real, numer_imag]), density), ("tile", "band", "pos")
    )
    probe_new = probe_planes + sum_numer / (sum_density + 1.0)
    return (object_new, probe_new)


def solution(mesh):
    in_specs = (
        P(None, "tile", "band"),
        P(),
        P("tile", "band", "pos", None, None, None),
        P("tile", "band", "pos", None, None),
        P("tile", "band", "pos"),
    )
    out_specs = (P(None, "tile", "band"), P())
    return jax.shard_map(
        on_device, mesh=mesh, in_specs=in_specs, out_specs=out_specs, check_vma=False
    )
```

profile of v0, /device:TPU:2, one launch (start us, length us, event | category | flops | bytes accessed | tf_op | source)
XLA Modules:
  0.0 733.1 jit_solution(11217168582069033955)
XLA Ops:
  7.2 8.0 %collective-permute-start = (f32[2,256,256]{2,1,0:T(8,128)}, f32[2,256,256]{2,1,0:T(8,128)S(1)}, u32[]{:S(2)}, u32[]{:S(2)}) collective-permute-start(f32[2,256,256]{2,1,0:T(8,128)} %param.13), channel_id=1, source_target_pairs={{4,0},{8,4},{12,8},{5,1},{9,5},{13,9},{6,2},{10,6},{14,10},{7,3},{... | collective-permute-start | bytes 1572872 | tf_op jit(solution)/shard_map/ppermute | solution.py:13
  15.2 1.1 constant_dynamic-update-slice_fusion.1
  16.3 6.8 collective-permute-done
  23.2 1.3 collective-permute-start.1
  24.5 0.6 fusion.170
  37.3 1.0 fusion.63
  38.5 1.0 copy-done
  39.5 3.7 fusion.16
  43.2 3.7 fusion.31
  46.9 4.1 fusion.8
  51.0 3.6 fusion.10
  54.6 3.7 fusion.17
  58.3 3.7 fusion.30
  62.0 3.8 fusion.20
  65.9 3.8 add_reduce_fusion.1
  69.6 0.3 bitcast_multiply_fusion.2
  69.9 3.6 fusion.36
  73.5 3.8 fusion.32
  77.3 3.6 multiply_subtract_fusion
  80.9 3.6 fusion
  84.6 4.0 fusion.2
  88.6 3.6 multiply_add_fusion
  92.2 3.9 add_subtract_fusion
  96.2 6.0 multiply_reduce_fusion.1
  102.1 0.3 bitcast_multiply_fusion.1
  102.4 0.2 pad_maximum_fusion
  102.6 1.0 slice_bitcast_fusion.2
  103.6 0.7 copy-done.4
  104.3 0.4 broadcast_in_dim.2
  104.7 10.4 %dynamic_update_slice.9 = f32[3,512,512]{2,1,0:T(8,128)S(1)} dynamic-update-slice(f32[3,512,512]{2,1,0:T(8,128)S(1)} %broadcast_in_dim.2, f32[3,256,256]{2,1,0:T(8,128)} %slice_bitcast_fusion.2, s32[]{:T(128)} %constant.88.clone.1, s32[]{:T(128)S(6)} %select_n.65, s32[]{:T(128)S(6)} %select_n.66) | dynamic-update-slice | bytes 1572868 | tf_op jit(solution)/shard_map/dynamic_update_slice | solution.py:89
  115.1 2.3 fusion.39
  117.4 10.9 %dynamic_update_slice.10 = f32[3,512,512]{2,1,0:T(8,128)S(1)} dynamic-update-slice(f32[3,512,512]{2,1,0:T(8,128)S(1)} %dynamic_update_slice.9, f32[3,256,256]{2,1,0:T(8,128)} %fusion.39, s32[]{:T(128)} %constant.88.clone.1, s32[]{:T(128)S(6)} %select_n.67, s32[]{:T(128)S(6)} %select_n.68) | dynamic-update-slice | bytes 1572868 | tf_op jit(solution)/shard_map/dynamic_update_slice | solution.py:89
  128.2 2.3 fusion.38
  130.5 10.2 %dynamic_update_slice.11 = f32[3,512,512]{2,1,0:T(8,128)S(1)} dynamic-update-slice(f32[3,512,512]{2,1,0:T(8,128)S(1)} %dynamic_update_slice.10, f32[3,256,256]{2,1,0:T(8,128)} %fusion.38, s32[]{:T(128)} %constant.88.clone.1, s32[]{:T(128)S(6)} %select_n.69, s32[]{:T(128)S(6)} %select_n.70) | dynamic-update-slice | bytes 1572868 | tf_op jit(solution)/shard_map/dynamic_update_slice | solution.py:89
  140.8 0.2 slice.130
  141.0 7.9 %collective-permute-start.2 = (f32[3,512,256]{2,1,0:T(8,128)S(1)}, f32[3,512,256]{2,1,0:T(8,128)S(1)}, u32[]{:S(2)}, u32[]{:S(2)}) collective-permute-start(f32[3,512,256]{2,1,0:T(8,128)S(1)} %slice.130), channel_id=1, source_target_pairs={{0,4},{4,8},{8,12},{1,5},{5,9},{9,13},{2,6},{6,10},{10,14},{3,7},{... | collective-permute-start | bytes 4718600 | tf_op jit(solution)/shard_map/ppermute | solution.py:13
  148.8 34.4 %collective-permute-done.2 = f32[3,512,256]{2,1,0:T(8,128)S(1)} collective-permute-done((f32[3,512,256]{2,1,0:T(8,128)S(1)}, f32[3,512,256]{2,1,0:T(8,128)S(1)}, u32[]{:S(2)}, u32[]{:S(2)}) %collective-permute-start.2) | collective-permute-done | bytes 1572896 | tf_op jit(solution)/shard_map/ppermute | solution.py:13
  183.2 0.3 slice_add_fusion
  183.6 2.7 collective-permute-start.3
  186.3 1.0 pad_maximum_fusion.2
  187.4 0.9 multiply_reduce_fusion.2
  188.3 2.2 slice_add_fusion.1
  190.6 472.6 %all-reduce.6.cloned.1.call-done = (f32[2,2,256,256]{3,2,1,0:T(8,128)}, f32[256,256]{1,0:T(8,128)}) async-done(((f32[2,2,256,256]{3,2,1,0:T(8,128)}, f32[256,256]{1,0:T(8,128)}), (f32[2,2,256,256]{3,2,1,0:T(8,128)}, f32[256,256]{1,0:T(8,128)})) %all-reduce.6.cloned.1.call-update) | async-done | bytes 1310736 | tf_op jit(solution)/shard_map/psum | solution.py:101
  663.2 1.0 broadcast_add_fusion
  664.2 2.4 divide_add_fusion
  666.6 56.5 %all-reduce.4.cloned.1.call-done = f32[3,256,256]{2,1,0:T(8,128)} async-done(((f32[3,256,256]{2,1,0:T(8,128)}), f32[3,256,256]{2,1,0:T(8,128)}) %all-reduce.4.cloned.1.call-update) | async-done | bytes 786448 | tf_op jit(solution)/shard_map/psum | solution.py:98
  723.1 1.0 fusion.70
  724.1 1.9 fusion.66
  (33 shorter events, 0.6 us)
Async XLA Ops:
  7.2 17.3 %copy-start.10 = (s32[1,1,1,3,2]{3,4,2,1,0:T(2,128)S(1)}, s32[1,1,1,3,2]{3,4,2,1,0:T(2,128)}, u32[]{:S(2)}) copy-start(s32[1,1,1,3,2]{3,4,2,1,0:T(2,128)} %param.16) | copy-start | bytes 76
  7.2 29.9 %copy-start.2 = (f32[2,2,256,256]{3,2,1,0:T(8,128)S(1)}, f32[2,2,256,256]{3,2,1,0:T(8,128)}, u32[]{:S(2)}) copy-start(f32[2,2,256,256]{3,2,1,0:T(8,128)} %param.14) | copy-start | bytes 3145732
  7.2 656.0 %all-reduce.6.cloned.1.call-start = ((), (), s32[]{:S(2)}) async-start(), calls=%async_computation.1 | async-start | bytes 2621440 | tf_op jit(solution)/shard_map/psum | solution.py:101
  7.2 15.9 %collective-permute-start = (f32[2,256,256]{2,1,0:T(8,128)}, f32[2,256,256]{2,1,0:T(8,128)S(1)}, u32[]{:S(2)}, u32[]{:S(2)}) collective-permute-start(f32[2,256,256]{2,1,0:T(8,128)} %param.13), channel_id=1, source_target_pairs={{4,0},{8,4},{12,8},{5,1},{9,5},{13,9},{6,2},{10,6},{14,10},{7,3},{... | collective-permute-start | bytes 1572872 | tf_op jit(solution)/shard_map/ppermute | solution.py:13
  23.2 14.1 %collective-permute-start.1 = (f32[2,256,512]{2,1,0:T(8,128)S(1)}, f32[2,256,512]{2,1,0:T(8,128)S(1)}, u32[]{:S(2)}, u32[]{:S(2)}) collective-permute-start(f32[2,256,512]{2,1,0:T(8,128)S(1)} %constant_dynamic-update-slice_fusion), channel_id=1, source_target_pairs={{16,0},{32,16},{48,32},{64,48},{80,64},{96,80},{112,96},{128,112},... | collective-permute-start | bytes 3145736 | tf_op jit(solution)/shard_map/ppermute | solution.py:13
  38.3 1.1 copy-start
  65.8 3.8 copy-start.7
  102.6 1.7 copy-start.4
  141.0 42.3 %collective-permute-start.2 = (f32[3,512,256]{2,1,0:T(8,128)S(1)}, f32[3,512,256]{2,1,0:T(8,128)S(1)}, u32[]{:S(2)}, u32[]{:S(2)}) collective-permute-start(f32[3,512,256]{2,1,0:T(8,128)S(1)} %slice.130), channel_id=1, source_target_pairs={{0,4},{4,8},{8,12},{1,5},{5,9},{9,13},{2,6},{6,10},{10,14},{3,7},{... | collective-permute-start | bytes 4718600 | tf_op jit(solution)/shard_map/ppermute | solution.py:13
  183.2 3.1 copy-start.8
  183.2 3.1 copy-start.9
  183.5 3.9 copy-start.5
  183.5 3.9 copy-start.1
  183.6 4.7 collective-permute-start.3
  188.3 475.9 %copy-start.3 = (f32[2,2,256,256]{3,2,1,0:T(8,128)S(1)}, f32[2,2,256,256]{3,2,1,0:T(8,128)}, u32[]{:S(2)}) copy-start(f32[2,2,256,256]{3,2,1,0:T(8,128)} %param.14) | copy-start | bytes 3145732
  188.3 534.9 %all-reduce.4.cloned.1.call-start = ((), (), s32[]{:S(2)}) async-start(), calls=%async_computation | async-start | bytes 1572864 | tf_op jit(solution)/shard_map/psum | solution.py:98
  664.2 59.9 %copy-start.6 = (f32[2,256,256]{2,1,0:T(8,128)S(1)}, f32[2,256,256]{2,1,0:T(8,128)}, u32[]{:S(2)}) copy-start(f32[2,256,256]{2,1,0:T(8,128)} %param.13) | copy-start | bytes 1572868
Sparse Core Ops, SparseCore 0:
  188.4 474.7 all-reduce.5
  665.6 57.5 all-reduce.3
where the time goes:
time: 743 us; the launch traced here: 733 us
  waiting for transfers between devices  570 us (77%)
  matrix products  62.2 us (8%)
  local copies, waits for them, and re-layouts  36.8 us (5%)
  between operations  26.6 us (4%)
  starting transfers between devices  19.9 us (3%)
  other arithmetic  17.1 us (2%)
    psum x1, waiting for transfers between devices, on_device(): lax.psum((jnp.stack([numer_real, numer_imag]), density), ('tile', 'band',...  473 us
    psum x1, waiting for transfers between devices, on_device(): tile_total = lax.psum(tile_core, 'pos')  56.5 us
    ppermute x4, waiting for transfers between devices, shifted(): return lax.ppermute(block, axis, route)  41.2 us
    dynamic_update_slice x3, local copies, waits for them, and re-layouts, on_device(): lax.dynamic_update_slice(running, previous + contributions[number], corne...  31.5 us
    ppermute x4, starting transfers between devices, shifted(): return lax.ppermute(block, axis, route)  19.8 us
  transfers between devices with their start and end apart: 6, of which 4 were waited for; matrix products, arithmetic and copies ran while one was open for 1% of the time, Pallas kernels for 0%

commit v1 on v0

--- a/solution.py
+++ b/solution.py
@@ -3,6 +3,7 @@
 import jax.numpy as jnp
 from jax import lax
 from jax.sharding import PartitionSpec as P
+from jax.lax import psum
 
 precise = lax.Precision.HIGHEST
 
@@ -98,9 +99,8 @@
     tile_total = lax.psum(tile_core, "pos")
     tile_light = tile_total[2]
     object_new = object_planes + tile_total[:2] / (tile_light + 1.0)
-    sum_numer, sum_density = lax.psum(
-        (jnp.stack([numer_real, numer_imag]), density), ("tile", "band", "pos")
-    )
+    _load_flows = lambda xin: psum(psum(xin, "tile"), ("band", "pos"))
+    sum_numer, sum_density = _load_flows((jnp.stack([numer_real, numer_imag]), density))
     probe_new = probe_planes + sum_numer / (sum_density + 1.0)
     return (object_new, probe_new)
 

time: 743 us -> 576 us (0.78)
  waiting for transfers between devices: 570 us -> 403 us
    psum x1 -> x2, waiting for transfers between devices: 473 us -> 335 us  [on_device(): _load_flows = lambda xin: psum(psum(xin, 'tile'), ('band', 'pos'))]
    ppermute x4, waiting for transfers between devices: 41.2 us -> 8.67 us  [shifted(): return lax.ppermute(block, axis, route)]
  transfers between devices with their start and end apart: 6 -> 7, of which waited for: 4 -> 5; matrix products, arithmetic and copies ran while one was open for 1% -> 2% of each run, Pallas kernels for 0% -> 0%
where the time goes in v1:
time: 576 us; the launch traced here: 566 us
  waiting for transfers between devices  403 us (70%)
  matrix products  62.2 us (11%)
  local copies, waits for them, and re-layouts  38 us (7%)
  between operations  26.2 us (5%)
  starting transfers between devices  19.6 us (3%)
  other arithmetic  17.3 us (3%)
    psum x2, waiting for transfers between devices, on_device(): _load_flows = lambda xin: psum(psum(xin, 'tile'), ('band', 'pos'))  335 us
    psum x1, waiting for transfers between devices, on_device(): tile_total = lax.psum(tile_core, 'pos')  58.7 us
    dynamic_update_slice x3, local copies, waits for them, and re-layouts, on_device(): lax.dynamic_update_slice(running, previous + contributions[number], corne...  31.5 us
    ppermute x4, starting transfers between devices, shifted(): return lax.ppermute(block, axis, route)  19.5 us
  transfers between devices with their start and end apart: 7, of which 5 were waited for; matrix products, arithmetic and copies ran while one was open for 2% of the time, Pallas kernels for 0%

profile of v1, /device:TPU:2, one launch (start us, length us, event | category | flops | bytes accessed | tf_op | source)
XLA Modules:
  0.0 566.0 jit_solution(714760384071132590)
XLA Ops:
  7.2 8.0 %collective-permute-start = (f32[2,256,256]{2,1,0:T(8,128)}, f32[2,256,256]{2,1,0:T(8,128)S(1)}, u32[]{:S(2)}, u32[]{:S(2)}) collective-permute-start(f32[2,256,256]{2,1,0:T(8,128)} %param.13), channel_id=1, source_target_pairs={{4,0},{8,4},{12,8},{5,1},{9,5},{13,9},{6,2},{10,6},{14,10},{7,3},{... | collective-permute-start | bytes 1572872 | tf_op jit(solution)/shard_map/ppermute | solution.py:14
  15.2 1.1 constant_dynamic-update-slice_fusion.1
  16.3 6.8 %collective-permute-done = f32[2,256,256]{2,1,0:T(8,128)S(1)} collective-permute-done((f32[2,256,256]{2,1,0:T(8,128)}, f32[2,256,256]{2,1,0:T(8,128)S(1)}, u32[]{:S(2)}, u32[]{:S(2)}) %collective-permute-start) | collective-permute-done | bytes 524320 | tf_op jit(solution)/shard_map/ppermute | solution.py:14
  23.2 1.3 collective-permute-start.1
  24.5 0.7 fusion.170
  37.2 1.0 fusion.63
  38.4 1.0 copy-done
  39.4 3.7 fusion.16
  43.1 3.7 fusion.31
  46.8 4.1 fusion.8
  50.9 3.6 fusion.10
  54.5 3.7 fusion.17
  58.2 3.7 fusion.30
  61.9 3.8 fusion.20
  65.8 3.8 add_reduce_fusion.1
  69.6 0.3 bitcast_multiply_fusion.2
  69.8 3.6 fusion.36
  73.4 3.8 fusion.32
  77.2 3.6 multiply_subtract_fusion
  80.8 3.6 fusion
  84.5 4.0 fusion.2
  88.5 3.6 multiply_add_fusion
  92.1 3.9 add_subtract_fusion
  96.1 6.0 %multiply_reduce_fusion.1 = (f32[2,256,256]{2,1,0:T(8,128)}, f32[2,256,256]{2,1,0:T(8,128)}, f32[3,256,256]{2,1,0:T(8,128)S(1)}, f32[3,256,256]{2,1,0:T(8,128)S(1)}) fusion(f32[3,2,256,256]{3,2,1,0:T(8,128)S(1)} %add_subtract_fusion, f32[3]{0:T(128)S(1)} %compare_convert_fusion, f32[3,256,256]{2,1,0:T(8,128)S(1)} %get-tuple-element.56, ...), kind=kOutput, calls=%fused_computation.26 | convolution fusion | flops 1217724416 | bytes 9961484 | tf_op jit(solution)/shard_map/nmij,jk->nmik/dot_general | solution.py:37
  102.1 0.3 bitcast_multiply_fusion.1
  102.5 1.0 slice_bitcast_fusion.2
  103.5 0.7 copy-done.4
  104.2 0.4 broadcast_in_dim.2
  104.6 10.4 %dynamic_update_slice.9 = f32[3,512,512]{2,1,0:T(8,128)S(1)} dynamic-update-slice(f32[3,512,512]{2,1,0:T(8,128)S(1)} %broadcast_in_dim.2, f32[3,256,256]{2,1,0:T(8,128)} %slice_bitcast_fusion.2, s32[]{:T(128)} %constant.88.clone.1, s32[]{:T(128)S(6)} %select_n.65, s32[]{:T(128)S(6)} %select_n.66) | dynamic-update-slice | bytes 1572868 | tf_op jit(solution)/shard_map/dynamic_update_slice | solution.py:90
  115.0 2.3 fusion.39
  117.3 10.9 %dynamic_update_slice.10 = f32[3,512,512]{2,1,0:T(8,128)S(1)} dynamic-update-slice(f32[3,512,512]{2,1,0:T(8,128)S(1)} %dynamic_update_slice.9, f32[3,256,256]{2,1,0:T(8,128)} %fusion.39, s32[]{:T(128)} %constant.88.clone.1, s32[]{:T(128)S(6)} %select_n.67, s32[]{:T(128)S(6)} %select_n.68) | dynamic-update-slice | bytes 1572868 | tf_op jit(solution)/shard_map/dynamic_update_slice | solution.py:90
  128.1 2.3 fusion.38
  130.4 10.2 %dynamic_update_slice.11 = f32[3,512,512]{2,1,0:T(8,128)S(1)} dynamic-update-slice(f32[3,512,512]{2,1,0:T(8,128)S(1)} %dynamic_update_slice.10, f32[3,256,256]{2,1,0:T(8,128)} %fusion.38, s32[]{:T(128)} %constant.88.clone.1, s32[]{:T(128)S(6)} %select_n.69, s32[]{:T(128)S(6)} %select_n.70) | dynamic-update-slice | bytes 1572868 | tf_op jit(solution)/shard_map/dynamic_update_slice | solution.py:90
  140.7 1.3 slice.130
  142.0 8.0 %collective-permute-start.2 = (f32[3,512,256]{2,1,0:T(8,128)}, f32[3,512,256]{2,1,0:T(8,128)}, u32[]{:S(2)}, u32[]{:S(2)}) collective-permute-start(f32[3,512,256]{2,1,0:T(8,128)} %slice.130), channel_id=1, source_target_pairs={{0,4},{4,8},{8,12},{1,5},{5,9},{9,13},{2,6},{6,10},{10,14},{3,7},{... | collective-permute-start | bytes 4718600 | tf_op jit(solution)/shard_map/ppermute | solution.py:14
  150.1 1.0 pad_maximum_fusion.2
  151.1 0.9 multiply_reduce_fusion.2
  152.0 220.2 %all-reduce.8.cloned.1.call-done = (f32[2,2,256,256]{3,2,1,0:T(8,128)}, f32[256,256]{1,0:T(8,128)}) async-done(((f32[2,2,256,256]{3,2,1,0:T(8,128)}, f32[256,256]{1,0:T(8,128)}), (f32[2,2,256,256]{3,2,1,0:T(8,128)}, f32[256,256]{1,0:T(8,128)})) %all-reduce.8.cloned.1.call-update) | async-done | bytes 1310736 | tf_op jit(solution)/shard_map/psum | solution.py:102
  372.3 1.7 slice_add_fusion
  374.1 2.2 collective-permute-start.3
  376.3 1.8 collective-permute-done.3
  378.1 1.0 slice_add_fusion.1
  379.2 115.1 %all-reduce.10.cloned.1.call-done = (f32[2,2,256,256]{3,2,1,0:T(8,128)}, f32[256,256]{1,0:T(8,128)}) async-done(((f32[2,2,256,256]{3,2,1,0:T(8,128)}, f32[256,256]{1,0:T(8,128)}), (f32[2,2,256,256]{3,2,1,0:T(8,128)}, f32[256,256]{1,0:T(8,128)})) %all-reduce.10.cloned.1.call-update) | async-done | bytes 1310736 | tf_op jit(solution)/shard_map/psum | solution.py:102
  494.2 1.0 broadcast_add_fusion
  495.2 2.4 divide_add_fusion
  497.6 58.7 %all-reduce.6.cloned.1.call-done = f32[3,256,256]{2,1,0:T(8,128)} async-done(((f32[3,256,256]{2,1,0:T(8,128)}), f32[3,256,256]{2,1,0:T(8,128)}) %all-reduce.6.cloned.1.call-update) | async-done | bytes 786448 | tf_op jit(solution)/shard_map/psum | solution.py:99
  556.3 1.0 fusion.70
  557.3 1.9 fusion.66
  (34 shorter events, 0.8 us)
Async XLA Ops:
  7.2 17.3 %copy-start.9 = (s32[1,1,1,3,2]{3,4,2,1,0:T(2,128)S(1)}, s32[1,1,1,3,2]{3,4,2,1,0:T(2,128)}, u32[]{:S(2)}) copy-start(s32[1,1,1,3,2]{3,4,2,1,0:T(2,128)} %param.16) | copy-start | bytes 76
  7.2 29.8 %copy-start.2 = (f32[2,2,256,256]{3,2,1,0:T(8,128)S(1)}, f32[2,2,256,256]{3,2,1,0:T(8,128)}, u32[]{:S(2)}) copy-start(f32[2,2,256,256]{3,2,1,0:T(8,128)} %param.14) | copy-start | bytes 3145732
  7.2 365.0 %all-reduce.8.cloned.1.call-start = ((), (), s32[]{:S(2)}) async-start(), calls=%async_computation.1 | async-start | bytes 2621440 | tf_op jit(solution)/shard_map/psum | solution.py:102
  7.2 15.9 %collective-permute-start = (f32[2,256,256]{2,1,0:T(8,128)}, f32[2,256,256]{2,1,0:T(8,128)S(1)}, u32[]{:S(2)}, u32[]{:S(2)}) collective-permute-start(f32[2,256,256]{2,1,0:T(8,128)} %param.13), channel_id=1, source_target_pairs={{4,0},{8,4},{12,8},{5,1},{9,5},{13,9},{6,2},{10,6},{14,10},{7,3},{... | collective-permute-start | bytes 1572872 | tf_op jit(solution)/shard_map/ppermute | solution.py:14
  23.2 14.0 %collective-permute-start.1 = (f32[2,256,512]{2,1,0:T(8,128)S(1)}, f32[2,256,512]{2,1,0:T(8,128)S(1)}, u32[]{:S(2)}, u32[]{:S(2)}) collective-permute-start(f32[2,256,512]{2,1,0:T(8,128)S(1)} %constant_dynamic-update-slice_fusion), channel_id=1, source_target_pairs={{16,0},{32,16},{48,32},{64,48},{80,64},{96,80},{112,96},{128,112},... | collective-permute-start | bytes 3145736 | tf_op jit(solution)/shard_map/ppermute | solution.py:14
  38.3 1.1 copy-start
  65.8 3.8 copy-start.6
  102.5 1.7 copy-start.4
  140.7 9.4 %copy-start.7 = (f32[2,256,256]{2,1,0:T(8,128)S(1)}, f32[2,256,256]{2,1,0:T(8,128)}, u32[]{:S(2)}) copy-start(f32[2,256,256]{2,1,0:T(8,128)} %get-tuple-element.42) | copy-start | bytes 1572868
  140.7 9.4 %copy-start.8 = (f32[2,256,256]{2,1,0:T(8,128)S(1)}, f32[2,256,256]{2,1,0:T(8,128)}, u32[]{:S(2)}) copy-start(f32[2,256,256]{2,1,0:T(8,128)} %get-tuple-element.43) | copy-start | bytes 1572868
  142.0 9.1 %copy-start.1 = (f32[3,2,256,256]{3,2,0,1:T(8,128)S(1)}, f32[3,2,256,256]{3,2,0,1:T(8,128)}, u32[]{:S(2)}) copy-start(f32[3,2,256,256]{3,2,0,1:T(8,128)} %copy-done) | copy-start | bytes 4718596
  142.0 230.2 %collective-permute-start.2 = (f32[3,512,256]{2,1,0:T(8,128)}, f32[3,512,256]{2,1,0:T(8,128)}, u32[]{:S(2)}, u32[]{:S(2)}) collective-permute-start(f32[3,512,256]{2,1,0:T(8,128)} %slice.130), channel_id=1, source_target_pairs={{0,4},{4,8},{8,12},{1,5},{5,9},{9,13},{2,6},{6,10},{10,14},{3,7},{... | collective-permute-start | bytes 4718600 | tf_op jit(solution)/shard_map/ppermute | solution.py:14
  152.0 342.3 %all-reduce.10.cloned.1.call-start = ((), (), s32[]{:S(2)}) async-start(), calls=%async_computation.2 | async-start | bytes 2621440 | tf_op jit(solution)/shard_map/psum | solution.py:102
  372.2 184.1 %all-reduce.6.cloned.1.call-start = ((), (), s32[]{:S(2)}) async-start(), calls=%async_computation | async-start | bytes 1572864 | tf_op jit(solution)/shard_map/psum | solution.py:99
  374.0 121.2 %copy-start.3 = (f32[2,2,256,256]{3,2,1,0:T(8,128)S(1)}, f32[2,2,256,256]{3,2,1,0:T(8,128)}, u32[]{:S(2)}) copy-start(f32[2,2,256,256]{3,2,1,0:T(8,128)} %param.14) | copy-start | bytes 3145732
  374.1 4.1 collective-permute-start.3
  495.2 62.1 %copy-start.5 = (f32[2,256,256]{2,1,0:T(8,128)S(1)}, f32[2,256,256]{2,1,0:T(8,128)}, u32[]{:S(2)}) copy-start(f32[2,256,256]{2,1,0:T(8,128)} %param.13) | copy-start | bytes 1572868
Sparse Core Ops, SparseCore 0:
  152.1 220.0 all-reduce.7
  375.9 118.3 all-reduce.9
  496.7 59.5 all-reduce.5
